TPU v7x, 32 devices: a whole 2x2x4 slice. The times are simulated.
32 devices in a mesh: row: 8 (over y, x, core), col: 4 (over z).
Axes of the slice: x: 2, y: 2, z: 4, core: 2. Of those that a mesh axis runs over, the one named last changes fastest.
Arguments:
- near_blocks: float32 [8, 16, 512, 512], P('row', 'col'), as said below
- leaf_bases: float32 [8, 512, 512], P('row'), may hold values from -1 to 1, as said below
- upper_bases: float32 [4, 256, 256], P('col'), may hold values from -1 to 1, as said below
- near_list: int32 [8, 16], P('row'), may hold values from 0 to 7, as said below
Outputs:
- factors: float32 [3072, 384], P('row')
- skeleton: float32 [1024, 1024], P('row', 'col')
- upper_skeleton: float32 [512, 512], P('row', 'col')
Inputs may be any that keep to these rules, and one draw needn't show every extreme that they name: `near_list`: entry 0 of row i is i; every entry of row i lies within 2 of i; entries may repeat. near_blocks[i, k] is the tile between leaf i and leaf near_list[i, k] of a symmetric matrix: a kernel matrix of points, a positive diagonal noise term and independent symmetric random entries; entries naming the same leaf hold equal tiles; every diagonal tile is symmetric positive definite. Each leaf_bases[i] is orthogonal. Each upper_bases[p] is orthogonal.
All inputs are finite; a program needn't handle non-finite values.
Results may differ from a plain program's by a relative error of at most 0.0003.
Values sent between devices are 32-bit elements; how exact they have to be, the bound alone decides.
A program may use at most 64 MiB of HBM per device.

v0:
```python
import functools

import jax
import jax.numpy as jnp
from jax import lax
from jax.experimental import pallas as pl
from jax.experimental.pallas import tpu as pltpu
from jax.sharding import PartitionSpec as P

SKEL = 128
REACH = 2
BLK = 128
PANEL = 8
F32 = jnp.float32
BF16 = jnp.bfloat16


def split(x):
    hi = x.astype(BF16)
    lo = (x - hi.astype(F32)).astype(BF16)
    return hi, lo


def mm(left, right, dims):
    lh, ll = split(left)
    rh, rl = split(right)
    dot = functools.partial(
        lax.dot_general, dimension_numbers=(dims, ((), ())), preferred_element_type=F32
    )
    return dot(lh, rh) + (dot(lh, rl) + dot(ll, rh))


NN = ((1,), (0,))
TN = ((0,), (0,))
NT = ((1,), (1,))


def panel_step(rows, base):
    width = rows.shape[1]
    sub = lax.broadcasted_iota(jnp.int32, (PANEL, 128), 0)
    cols = [
        jnp.broadcast_to(rows[:, base + t : base + t + 1], (PANEL, 128)) for t in range(PANEL)
    ]
    parts = [rows[:, c : c + 128] for c in range(0, width, 128)]
    for t in range(PANEL):
        scale = lax.rsqrt(cols[t][t : t + 1, :])
        mult = jnp.where(sub > t, cols[t] * scale, 0.0)
        for u in range(t + 1, PANEL):
            cols[u] = cols[u] - mult * (cols[u][t : t + 1, :] * scale)
        for c in range(len(parts)):
            lead = parts[c][t : t + 1, :] * scale
            parts[c] = jnp.where(sub == t, lead, parts[c] - mult * lead)
    return jnp.concatenate(parts, axis=1)


def chol_inv(work):
    for base in range(0, BLK, PANEL):
        rows = panel_step(work[base : base + PANEL, :], base)
        work[base : base + PANEL, :] = rows
        rest = BLK - base - PANEL
        if rest:
            high = rows.astype(BF16).astype(F32)
            low = rows - high
            left = jnp.concatenate([high, high, low, low], axis=0)[:, :BLK].astype(BF16)
            right = jnp.concatenate([high, low, high, low], axis=0).astype(BF16)
            update = lax.dot_general(
                left, right, (TN, ((), ())), preferred_element_type=F32
            )
            work[base + PANEL :, :] = work[base + PANEL :, :] - update[base + PANEL :, :]


def load_block(work, block):
    row = lax.broadcasted_iota(jnp.int32, (BLK, BLK), 0)
    col = lax.broadcasted_iota(jnp.int32, (BLK, BLK), 1)
    work[:, :BLK] = (block + block.T) * 0.5
    work[:, BLK:] = jnp.where(row == col, 1.0, 0.0)


def upper_part(block):
    row = lax.broadcasted_iota(jnp.int32, (BLK, BLK), 0)
    col = lax.broadcasted_iota(jnp.int32, (BLK, BLK), 1)
    return jnp.where(col >= row, block, 0.0)


def pivot_kernel(near_ref, basis_ref, factor_ref, combined_ref, mat, work):
    order = basis_ref.shape[0]
    red = order - SKEL
    count = red // BLK
    rotated = mm(basis_ref[:, :red], mm(near_ref[...], basis_ref[...], NN), TN)
    square = rotated[:, :red]
    mat[:, :red] = (square + square.T) * 0.5
    mat[:, red:] = rotated[:, red:]
    factor_ref[...] = jnp.zeros_like(factor_ref)
    inverses, leads = [], []
    for j in range(count):
        lo, hi = j * BLK, (j + 1) * BLK
        load_block(work, mat[lo:hi, lo:hi])
        chol_inv(work)
        factor_ref[lo:hi, lo:hi] = upper_part(work[:, :BLK]).T
        inverse = work[:, BLK:]
        lead = mm(inverse, mat[lo:hi, hi:], NN)
        if hi < red:
            factor_ref[hi:red, lo:hi] = lead[:, : red - hi].T
            mat[hi:red, hi:] = mat[hi:red, hi:] - mm(lead[:, : red - hi], lead, TN)
        inverses.append(inverse)
        leads.append(lead)
    folded = []
    for j in reversed(range(count)):
        rest = red - (j + 1) * BLK
        rhs = leads[j][:, rest:]
        if folded:
            rhs = rhs - mm(leads[j][:, :rest], jnp.concatenate(folded, axis=0), NN)
        folded.insert(0, mm(inverses[j], rhs, TN))
    combined_ref[...] = basis_ref[:, red:] - mm(
        basis_ref[:, :red], jnp.concatenate(folded, axis=0), NN
    )


def pivot(near_tile, basis):
    order = basis.shape[0]
    red = order - SKEL
    return pl.pallas_call(
        pivot_kernel,
        out_shape=(
            jax.ShapeDtypeStruct((red, red), F32),
            jax.ShapeDtypeStruct((order, SKEL), F32),
        ),
        in_specs=[pl.BlockSpec(memory_space=pltpu.VMEM)] * 2,
        out_specs=[pl.BlockSpec(memory_space=pltpu.VMEM)] * 2,
        scratch_shapes=[pltpu.VMEM((red, order), F32), pltpu.VMEM((BLK, 2 * BLK), F32)],
        compiler_params=pltpu.CompilerParams(vmem_limit_bytes=32 * 1024 * 1024),
        name="leaf_pivot",
    )(near_tile, basis)


def fold_kernel(rotated_ref, out_ref, work):
    load_block(work, rotated_ref[:SKEL, :SKEL])
    chol_inv(work)
    inverse = work[:, BLK:]
    out_ref[...] = mm(inverse, mm(inverse, rotated_ref[:SKEL, SKEL:], NN), TN)


def fold(rotated):
    return pl.pallas_call(
        fold_kernel,
        out_shape=jax.ShapeDtypeStruct((SKEL, SKEL), F32),
        in_specs=[pl.BlockSpec(memory_space=pltpu.VMEM)],
        out_specs=pl.BlockSpec(memory_space=pltpu.VMEM),
        scratch_shapes=[pltpu.VMEM((BLK, 2 * BLK), F32)],
        name="parent_pivot",
    )(rotated)


def spread(block, axis):
    step = lax.axis_size(axis) // 2
    index = lax.axis_index(axis)
    while step >= 1:
        pairs = [(i, i + step) for i in range(0, lax.axis_size(axis), 2 * step)]
        got = lax.ppermute(block, axis, pairs)
        block = jnp.where(index % (2 * step) == step, got, block)
        step //= 2
    return block


def from_behind(block, axis, distance):
    devices = range(lax.axis_size(axis))
    route = [(i - distance, i) for i in devices if i - distance in devices]
    return lax.ppermute(block, axis, route)


def swapped(value, axis, distance):
    mask = 2**distance
    pairs = [(source, source ^ mask) for source in range(lax.axis_size(axis))]
    return lax.ppermute(value, axis, pairs)


def product(left, right):
    return jnp.dot(left, right, precision=lax.Precision.HIGH)


def local(near_blocks, leaf_bases, upper_bases, near_list):
    leaf_order = leaf_bases.shape[1]
    red_count = leaf_order - SKEL
    entry_count = near_blocks.shape[1]
    row_index = lax.axis_index("row")
    col_index = lax.axis_index("col")
    row_slot = row_index % 2
    holder = row_index // 2
    own_basis = leaf_bases[0]
    near_row = near_list[0]
    parent_reach = (REACH + 1) // 2

    def blank_pivot(near_tile, basis):
        return (
            jnp.zeros((red_count, red_count), F32),
            jnp.zeros((leaf_order, SKEL), F32),
        )

    factor, combined = lax.cond(
        col_index == 0, pivot, blank_pivot, near_blocks[0, 0], own_basis
    )
    combined = spread(combined, "col")
    factor = spread(factor, "col")
    skel_basis_t = own_basis[:, red_count:].T
    row_products = []
    slot_list = []
    for entry in range(entry_count):
        row_products.append(product(skel_basis_t, near_blocks[0, entry]))
        col_leaf = lax.dynamic_index_in_dim(
            near_row, col_index * entry_count + entry, 0, keepdims=False
        )
        slot_list.append(col_leaf - row_index + REACH)
    tile_list = []
    combined_list = []
    for offset in range(-REACH, REACH + 1):
        if offset == 0:
            combined_list.append(combined)
        else:
            combined_list.append(from_behind(combined, "row", -offset))
    combined_table = jnp.stack(combined_list)
    for entry in range(entry_count):
        column_part = lax.dynamic_index_in_dim(combined_table, slot_list[entry], 0, keepdims=False)
        tile_list.append(product(row_products[entry], column_part))
    compact = jnp.stack(tile_list)
    gathered = lax.all_gather(compact, "col", axis=0, tiled=True)
    strips = []
    for column_slot in range(2):
        target_leaf = col_index * 2 + column_slot
        matches = near_row == target_leaf
        first_match = jnp.argmax(matches)
        picked = lax.dynamic_index_in_dim(gathered, first_match, 0, keepdims=False)
        strips.append(jnp.where(jnp.any(matches), picked, jnp.zeros_like(picked)))
    skeleton_strip = jnp.concatenate(strips, axis=1)
    partner = swapped(skeleton_strip, "row", 0)
    merged = jnp.where(
        row_slot == 0,
        jnp.concatenate([skeleton_strip, partner], axis=0),
        jnp.concatenate([partner, skeleton_strip], axis=0),
    )
    upper_basis = upper_bases[0]
    basis_pieces = []
    for offset in range(-parent_reach, parent_reach + 1):
        if offset == 0:
            basis_pieces.append(upper_basis)
        else:
            basis_pieces.append(from_behind(upper_basis, "col", -offset))
    parent_table = jnp.stack(basis_pieces)
    basis_slot = jnp.clip(holder - col_index + parent_reach, 0, 2 * parent_reach)
    parent_basis = lax.dynamic_index_in_dim(parent_table, basis_slot, 0, keepdims=False)
    parent_rotated = product(parent_basis.T, product(merged, upper_basis))
    folded = lax.cond(
        row_index == col_index * 2, fold, lambda block: jnp.zeros((SKEL, SKEL), F32), parent_rotated
    )
    pieces = []
    for offset in range(-2 * parent_reach - 1, 2 * parent_reach + 1):
        pieces.append(folded if offset == 0 else from_behind(folded, "row", -offset))
    pivot_slot = jnp.clip(2 * col_index - row_index + 2 * parent_reach + 1, 0, 4 * parent_reach + 1)
    chosen = lax.dynamic_index_in_dim(jnp.stack(pieces), pivot_slot, 0, keepdims=False)
    in_window = jnp.abs(holder - col_index) <= parent_reach
    chosen = jnp.where(in_window, chosen, jnp.zeros_like(chosen))
    low_rows = lax.dynamic_slice_in_dim(
        parent_rotated, SKEL + row_slot * (SKEL // 2), SKEL // 2, 0
    )
    upper_half = low_rows[:, SKEL:] - product(low_rows[:, :SKEL], chosen)
    return (factor, skeleton_strip, upper_half)


def solution(mesh):
    return jax.shard_map(
        local,
        mesh=mesh,
        in_specs=(
            P("row", "col", None, None),
            P("row", None, None),
            P("col", None, None),
            P("row", None),
        ),
        out_specs=(P("row", None), P("row", "col"), P("row", "col")),
        check_vma=False,
    )
```

profile of v0, /device:TPU:10, one launch (start us, length us, event | category | flops | bytes accessed | tf_op | source)
XLA Modules:
  0.0 163.5 jit_solution(5621614046360265903)
XLA Ops:
  7.2 1.4 slice_bitcast_fusion
  9.5 1.7 %fusion.4 = f32[128,512]{1,0:T(8,128)S(1)} fusion(f32[1,4,512,512]{3,2,1,0:T(8,128)} %param.8, f32[512,512]{1,0:T(8,128)S(1)} %bitcast.83), kind=kOutput, calls=%fused_computation.9 | convolution fusion | flops 201326592 | bytes 1572864 | tf_op jit(solution)/shard_map/dot_general | solution.py:178
  11.2 1.7 %fusion.35 = f32[128,512]{1,0:T(8,128)S(1)} fusion(f32[512,512]{1,0:T(8,128)S(1)} %bitcast.84, f32[1,4,512,512]{3,2,1,0:T(8,128)} %param.8), kind=kOutput, calls=%fused_computation.52 | convolution fusion | flops 201326592 | bytes 1572864 | tf_op jit(solution)/shard_map/dot_general | solution.py:178
  13.0 1.3 collective-permute-start.3
  14.3 1.7 %fusion.2 = f32[128,512]{1,0:T(8,128)S(1)} fusion(f32[1,4,512,512]{3,2,1,0:T(8,128)} %param.8, f32[512,512]{1,0:T(8,128)S(1)} %bitcast.85), kind=kOutput, calls=%fused_computation.7 | convolution fusion | flops 201326592 | bytes 1572864 | tf_op jit(solution)/shard_map/dot_general | solution.py:178
  16.0 27.5 %collective-permute-done.3 = f32[512,128]{1,0:T(8,128)S(1)} collective-permute-done((f32[512,128]{1,0:T(8,128)S(1)}, f32[512,128]{1,0:T(8,128)S(1)}, u32[]{:S(2)}, u32[]{:S(2)}) %collective-permute-start.3) | collective-permute-done | bytes 262176 | tf_op jit(solution)/shard_map/ppermute | solution.py:159
  43.5 3.4 %collective-permute-start.4 = (f32[512,128]{1,0:T(8,128)S(1)}, f32[512,128]{1,0:T(8,128)S(1)}, u32[]{:S(2)}, u32[]{:S(2)}) collective-permute-start(f32[512,128]{1,0:T(8,128)S(1)} %broadcast_select_fusion.3), channel_id=1, source_target_pairs={{0,8},{4,12},{8,16},{12,20},{16,24},{20,28},{1,9},{5,13},{9,17},{1... | collective-permute-start | bytes 786440 | tf_op jit(solution)/shard_map/ppermute | solution.py:168
  46.9 1.9 %collective-permute-start.5 = (f32[512,128]{1,0:T(8,128)S(1)}, f32[512,128]{1,0:T(8,128)S(1)}, u32[]{:S(2)}, u32[]{:S(2)}) collective-permute-start(f32[512,128]{1,0:T(8,128)S(1)} %broadcast_select_fusion.3), channel_id=1, source_target_pairs={{0,4},{4,8},{8,12},{12,16},{16,20},{20,24},{24,28},{1,5},{5,9},{9,... | collective-permute-start | bytes 786440 | tf_op jit(solution)/shard_map/ppermute | solution.py:168
  48.8 1.7 %fusion = f32[128,512]{1,0:T(8,128)S(1)} fusion(f32[1,4,512,512]{3,2,1,0:T(8,128)} %param.8, f32[512,512]{1,0:T(8,128)S(1)} %bitcast.86), kind=kOutput, calls=%fused_computation.5 | convolution fusion | flops 201326592 | bytes 1572864 | tf_op jit(solution)/shard_map/dot_general | solution.py:178
  53.8 3.6 %collective-permute-start.6 = (f32[512,128]{1,0:T(8,128)S(1)}, f32[512,128]{1,0:T(8,128)S(1)}, u32[]{:S(2)}, u32[]{:S(2)}) collective-permute-start(f32[512,128]{1,0:T(8,128)S(1)} %broadcast_select_fusion.3), channel_id=1, source_target_pairs={{4,0},{8,4},{12,8},{16,12},{20,16},{24,20},{28,24},{5,1},{9,5},{13... | collective-permute-start | bytes 786440 | tf_op jit(solution)/shard_map/ppermute | solution.py:168
  57.5 1.9 %collective-permute-start.7 = (f32[512,128]{1,0:T(8,128)S(1)}, f32[512,128]{1,0:T(8,128)S(1)}, u32[]{:S(2)}, u32[]{:S(2)}) collective-permute-start(f32[512,128]{1,0:T(8,128)S(1)} %broadcast_select_fusion.3), channel_id=1, source_target_pairs={{8,0},{12,4},{16,8},{20,12},{24,16},{28,20},{9,1},{13,5},{17,9},{2... | collective-permute-start | bytes 786440 | tf_op jit(solution)/shard_map/ppermute | solution.py:168
  59.5 3.2 %collective-permute-done.6 = f32[512,128]{1,0:T(8,128)S(1)} collective-permute-done((f32[512,128]{1,0:T(8,128)S(1)}, f32[512,128]{1,0:T(8,128)S(1)}, u32[]{:S(2)}, u32[]{:S(2)}) %collective-permute-start.6) | collective-permute-done | bytes 262176 | tf_op jit(solution)/shard_map/ppermute | solution.py:168
  62.8 7.0 %collective-permute-done.7 = f32[512,128]{1,0:T(8,128)S(1)} collective-permute-done((f32[512,128]{1,0:T(8,128)S(1)}, f32[512,128]{1,0:T(8,128)S(1)}, u32[]{:S(2)}, u32[]{:S(2)}) %collective-permute-start.7) | collective-permute-done | bytes 262176 | tf_op jit(solution)/shard_map/ppermute | solution.py:168
  70.9 0.7 pad_maximum_fusion
  71.7 1.0 collective-permute-start
  78.5 27.2 %all-gather.2.cloned.1.call-done = f32[16,128,128]{2,1,0:T(8,128)} async-done(((f32[4,128,128]{2,1,0:T(8,128)}), f32[16,128,128]{2,1,0:T(8,128)}) %all-gather.2.cloned.1.call-update) | async-done | bytes 1048592 | tf_op jit(solution)/shard_map/all_gather | solution.py:225
  105.8 2.2 %select_bitcast_fusion.1 = (f32[128,128]{1,0:T(8,128)S(1)}, f32[128,128]{1,0:T(8,128)S(1)}) fusion(f32[16,128,128]{2,1,0:T(8,128)} %all-gather.2.cloned.1.call-done, s32[]{:T(128)S(6)} %select_n.153, pred[]{:T(512)} %get-tuple-element.24, s32[]{:T(128)S(6)} %select_n.157, pred[]{:T(512)} %get-tuple-element.25), kind=kLoop, calls=%fused_computation.67 | loop fusion | flops 32768 | bytes 262154 | tf_op jit(solution)/shard_map/jit(_where)/select_n | solution.py:232
  108.2 1.3 collective-permute-start.1
  109.5 5.5 %collective-permute-start.8 = (f32[256,256]{1,0:T(8,128)S(1)}, f32[256,256]{1,0:T(8,128)S(1)}, u32[]{:S(2)}, u32[]{:S(2)}) collective-permute-start(f32[256,256]{1,0:T(8,128)S(1)} %bitcast.87), channel_id=1, source_target_pairs={{0,1},{1,2},{2,3},{4,5},{5,6},{6,7},{8,9},{9,10},{10,11},{12,13},{... | collective-permute-start | bytes 786440 | tf_op jit(solution)/shard_map/ppermute | solution.py:168
  115.0 1.9 %collective-permute-start.9 = (f32[256,256]{1,0:T(8,128)S(1)}, f32[256,256]{1,0:T(8,128)S(1)}, u32[]{:S(2)}, u32[]{:S(2)}) collective-permute-start(f32[256,256]{1,0:T(8,128)S(1)} %bitcast.88), channel_id=1, source_target_pairs={{1,0},{2,1},{3,2},{5,4},{6,5},{7,6},{9,8},{10,9},{11,10},{13,12},{... | collective-permute-start | bytes 786440 | tf_op jit(solution)/shard_map/ppermute | solution.py:168
  117.3 14.1 %collective-permute-done.8 = f32[256,256]{1,0:T(8,128)S(1)} collective-permute-done((f32[256,256]{1,0:T(8,128)S(1)}, f32[256,256]{1,0:T(8,128)S(1)}, u32[]{:S(2)}, u32[]{:S(2)}) %collective-permute-start.8) | collective-permute-done | bytes 262176 | tf_op jit(solution)/shard_map/ppermute | solution.py:168
  131.8 7.1 %conditional.3 = (f32[128,128]{1,0:T(8,128)}, f32[1,128,128]{2,1,0:T(8,128)S(1)}) conditional(s32[]{:T(128)} %convert_element_type.7, () %tuple.30, f32[256,256]{1,0:T(8,128)S(1)} %fusion.12), branch_computations={%region_6.7_spmd, %region_7.8_spmd} | conditional | bytes 131096 | solution.py:251
  131.8 6.3 %parent_pivot.1 = f32[128,128]{1,0:T(8,128)} custom-call(f32[256,256]{1,0:T(8,128)S(1)} %rotated_ref), custom_call_target="tpu_custom_call" | custom-call | tf_op jit(solution)/shard_map/cond/branch_1_fun/parent_pivot/pallas_call | solution.py:144
  138.1 0.8 copy.18
  138.9 1.3 collective-permute-start.11
  140.2 0.9 broadcast_select_fusion.1
  141.1 1.9 %collective-permute-start.12 = (f32[128,128]{1,0:T(8,128)}, f32[128,128]{1,0:T(8,128)S(1)}, u32[]{:S(2)}, u32[]{:S(2)}) collective-permute-start(f32[128,128]{1,0:T(8,128)} %get-tuple-element.22), channel_id=1, source_target_pairs={{0,8},{4,12},{8,16},{12,20},{16,24},{20,28},{1,9},{5,13},{9,17},{1... | collective-permute-start | bytes 196616 | tf_op jit(solution)/shard_map/ppermute | solution.py:168
  143.0 1.9 %collective-permute-start.13 = (f32[128,128]{1,0:T(8,128)}, f32[128,128]{1,0:T(8,128)S(1)}, u32[]{:S(2)}, u32[]{:S(2)}) collective-permute-start(f32[128,128]{1,0:T(8,128)} %get-tuple-element.22), channel_id=1, source_target_pairs={{0,4},{4,8},{8,12},{12,16},{16,20},{20,24},{24,28},{1,5},{5,9},{9,... | collective-permute-start | bytes 196616 | tf_op jit(solution)/shard_map/ppermute | solution.py:168
  144.9 3.6 %collective-permute-start.14 = (f32[128,128]{1,0:T(8,128)}, f32[128,128]{1,0:T(8,128)S(1)}, u32[]{:S(2)}, u32[]{:S(2)}) collective-permute-start(f32[128,128]{1,0:T(8,128)} %get-tuple-element.22), channel_id=1, source_target_pairs={{4,0},{8,4},{12,8},{16,12},{20,16},{24,20},{28,24},{5,1},{9,5},{13... | collective-permute-start | bytes 196616 | tf_op jit(solution)/shard_map/ppermute | solution.py:168
  148.6 1.9 %collective-permute-start.15 = (f32[128,128]{1,0:T(8,128)}, f32[128,128]{1,0:T(8,128)S(1)}, u32[]{:S(2)}, u32[]{:S(2)}) collective-permute-start(f32[128,128]{1,0:T(8,128)} %get-tuple-element.22), channel_id=1, source_target_pairs={{8,0},{12,4},{16,8},{20,12},{24,16},{28,20},{9,1},{13,5},{17,9},{2... | collective-permute-start | bytes 196616 | tf_op jit(solution)/shard_map/ppermute | solution.py:168
  150.8 5.1 %collective-permute-done.15 = f32[128,128]{1,0:T(8,128)S(1)} collective-permute-done((f32[128,128]{1,0:T(8,128)}, f32[128,128]{1,0:T(8,128)S(1)}, u32[]{:S(2)}, u32[]{:S(2)}) %collective-permute-start.15) | collective-permute-done | bytes 65568 | tf_op jit(solution)/shard_map/ppermute | solution.py:168
  155.9 0.8 convolution_subtract_fusion
  (51 shorter events, 6.0 us)
Async XLA Ops:
  7.2 1.5 copy-start
  7.2 98.6 %all-gather.2.cloned.1.call-start = ((), (), s32[]{:S(2)}) async-start(), calls=%async_computation | async-start | bytes 1310720 | tf_op jit(solution)/shard_map/all_gather | solution.py:225
  8.8 4.2 %collective-permute-start.2 = (f32[512,128]{1,0:T(8,128)S(1)}, f32[512,128]{1,0:T(8,128)S(1)}, u32[]{:S(2)}, u32[]{:S(2)}) collective-permute-start(f32[512,128]{1,0:T(8,128)S(1)} %get-tuple-element.19), channel_id=1, source_target_pairs={{0,2},{4,6},{8,10},{12,14},{16,18},{20,22},{24,26},{28,30}} | collective-permute-start | bytes 786440 | tf_op jit(solution)/shard_map/ppermute | solution.py:159
  13.0 30.5 %collective-permute-start.3 = (f32[512,128]{1,0:T(8,128)S(1)}, f32[512,128]{1,0:T(8,128)S(1)}, u32[]{:S(2)}, u32[]{:S(2)}) collective-permute-start(f32[512,128]{1,0:T(8,128)S(1)} %broadcast_select_fusion.2), channel_id=1, source_target_pairs={{0,1},{2,3},{4,5},{6,7},{8,9},{10,11},{12,13},{14,15},{16,17},{18,... | collective-permute-start | bytes 786440 | tf_op jit(solution)/shard_map/ppermute | solution.py:159
  16.0 34.6 %copy-start.3 = (s32[1,16]{1,0:T(1,128)S(1)}, s32[1,16]{1,0:T(1,128)}, u32[]{:S(2)}) copy-start(s32[1,16]{1,0:T(1,128)} %param.11) | copy-start | bytes 196
  43.5 15.9 %collective-permute-start.4 = (f32[512,128]{1,0:T(8,128)S(1)}, f32[512,128]{1,0:T(8,128)S(1)}, u32[]{:S(2)}, u32[]{:S(2)}) collective-permute-start(f32[512,128]{1,0:T(8,128)S(1)} %broadcast_select_fusion.3), channel_id=1, source_target_pairs={{0,8},{4,12},{8,16},{12,20},{16,24},{20,28},{1,9},{5,13},{9,17},{1... | collective-permute-start | bytes 786440 | tf_op jit(solution)/shard_map/ppermute | solution.py:168
  46.9 12.5 %collective-permute-start.5 = (f32[512,128]{1,0:T(8,128)S(1)}, f32[512,128]{1,0:T(8,128)S(1)}, u32[]{:S(2)}, u32[]{:S(2)}) collective-permute-start(f32[512,128]{1,0:T(8,128)S(1)} %broadcast_select_fusion.3), channel_id=1, source_target_pairs={{0,4},{4,8},{8,12},{12,16},{16,20},{20,24},{24,28},{1,5},{5,9},{9,... | collective-permute-start | bytes 786440 | tf_op jit(solution)/shard_map/ppermute | solution.py:168
  53.8 8.9 %collective-permute-start.6 = (f32[512,128]{1,0:T(8,128)S(1)}, f32[512,128]{1,0:T(8,128)S(1)}, u32[]{:S(2)}, u32[]{:S(2)}) collective-permute-start(f32[512,128]{1,0:T(8,128)S(1)} %broadcast_select_fusion.3), channel_id=1, source_target_pairs={{4,0},{8,4},{12,8},{16,12},{20,16},{24,20},{28,24},{5,1},{9,5},{13... | collective-permute-start | bytes 786440 | tf_op jit(solution)/shard_map/ppermute | solution.py:168
  57.5 12.3 %collective-permute-start.7 = (f32[512,128]{1,0:T(8,128)S(1)}, f32[512,128]{1,0:T(8,128)S(1)}, u32[]{:S(2)}, u32[]{:S(2)}) collective-permute-start(f32[512,128]{1,0:T(8,128)S(1)} %broadcast_select_fusion.3), channel_id=1, source_target_pairs={{8,0},{12,4},{16,8},{20,12},{24,16},{28,20},{9,1},{13,5},{17,9},{2... | collective-permute-start | bytes 786440 | tf_op jit(solution)/shard_map/ppermute | solution.py:168
  71.6 37.8 %copy-start.1 = (f32[1,256,256]{2,1,0:T(8,128)S(1)}, f32[1,256,256]{2,1,0:T(8,128)}, u32[]{:S(2)}) copy-start(f32[1,256,256]{2,1,0:T(8,128)} %param.10) | copy-start | bytes 786436
  71.7 36.4 %collective-permute-start = (f32[384,384]{1,0:T(8,128)S(1)}, f32[384,384]{1,0:T(8,128)S(1)}, u32[]{:S(2)}, u32[]{:S(2)}) collective-permute-start(f32[384,384]{1,0:T(8,128)S(1)} %get-tuple-element.18), channel_id=1, source_target_pairs={{0,2},{4,6},{8,10},{12,14},{16,18},{20,22},{24,26},{28,30}} | collective-permute-start | bytes 1769480 | tf_op jit(solution)/shard_map/ppermute | solution.py:159
  108.0 9.3 %copy-start.2 = (f32[128,256]{1,0:T(8,128)}, f32[128,256]{1,0:T(8,128)S(1)}, u32[]{:S(2)}) copy-start(f32[128,256]{1,0:T(8,128)S(1)} %pad_maximum_fusion.1) | copy-start | bytes 393220
  108.0 9.0 %collective-permute-start.10 = (f32[128,256]{1,0:T(8,128)S(1)}, f32[128,256]{1,0:T(8,128)S(1)}, u32[]{:S(2)}, u32[]{:S(2)}) collective-permute-start(f32[128,256]{1,0:T(8,128)S(1)} %pad_maximum_fusion.1), channel_id=1, source_target_pairs={{0,4},{4,0},{8,12},{12,8},{16,20},{20,16},{24,28},{28,24},{1,5},{5... | collective-permute-start | bytes 393224 | tf_op jit(solution)/shard_map/ppermute | solution.py:174
  108.2 32.0 %collective-permute-start.1 = (f32[384,384]{1,0:T(8,128)S(1)}, f32[384,384]{1,0:T(8,128)S(1)}, u32[]{:S(2)}, u32[]{:S(2)}) collective-permute-start(f32[384,384]{1,0:T(8,128)S(1)} %broadcast_select_fusion), channel_id=1, source_target_pairs={{0,1},{2,3},{4,5},{6,7},{8,9},{10,11},{12,13},{14,15},{16,17},{18,... | collective-permute-start | bytes 1769480 | tf_op jit(solution)/shard_map/ppermute | solution.py:159
  109.5 21.9 %collective-permute-start.8 = (f32[256,256]{1,0:T(8,128)S(1)}, f32[256,256]{1,0:T(8,128)S(1)}, u32[]{:S(2)}, u32[]{:S(2)}) collective-permute-start(f32[256,256]{1,0:T(8,128)S(1)} %bitcast.87), channel_id=1, source_target_pairs={{0,1},{1,2},{2,3},{4,5},{5,6},{6,7},{8,9},{9,10},{10,11},{12,13},{... | collective-permute-start | bytes 786440 | tf_op jit(solution)/shard_map/ppermute | solution.py:168
  115.0 16.4 %collective-permute-start.9 = (f32[256,256]{1,0:T(8,128)S(1)}, f32[256,256]{1,0:T(8,128)S(1)}, u32[]{:S(2)}, u32[]{:S(2)}) collective-permute-start(f32[256,256]{1,0:T(8,128)S(1)} %bitcast.88), channel_id=1, source_target_pairs={{1,0},{2,1},{3,2},{5,4},{6,5},{7,6},{9,8},{10,9},{11,10},{13,12},{... | collective-permute-start | bytes 786440 | tf_op jit(solution)/shard_map/ppermute | solution.py:168
  138.9 11.6 %collective-permute-start.11 = (f32[128,128]{1,0:T(8,128)}, f32[128,128]{1,0:T(8,128)S(1)}, u32[]{:S(2)}, u32[]{:S(2)}) collective-permute-start(f32[128,128]{1,0:T(8,128)} %get-tuple-element.22), channel_id=1, source_target_pairs={{0,12},{4,16},{8,20},{12,24},{16,28},{1,13},{5,17},{9,21},{13,25},... | collective-permute-start | bytes 196616 | tf_op jit(solution)/shard_map/ppermute | solution.py:168
  141.1 9.4 %collective-permute-start.12 = (f32[128,128]{1,0:T(8,128)}, f32[128,128]{1,0:T(8,128)S(1)}, u32[]{:S(2)}, u32[]{:S(2)}) collective-permute-start(f32[128,128]{1,0:T(8,128)} %get-tuple-element.22), channel_id=1, source_target_pairs={{0,8},{4,12},{8,16},{12,20},{16,24},{20,28},{1,9},{5,13},{9,17},{1... | collective-permute-start | bytes 196616 | tf_op jit(solution)/shard_map/ppermute | solution.py:168
  143.0 7.6 %collective-permute-start.13 = (f32[128,128]{1,0:T(8,128)}, f32[128,128]{1,0:T(8,128)S(1)}, u32[]{:S(2)}, u32[]{:S(2)}) collective-permute-start(f32[128,128]{1,0:T(8,128)} %get-tuple-element.22), channel_id=1, source_target_pairs={{0,4},{4,8},{8,12},{12,16},{16,20},{20,24},{24,28},{1,5},{5,9},{9,... | collective-permute-start | bytes 196616 | tf_op jit(solution)/shard_map/ppermute | solution.py:168
  144.9 5.8 %collective-permute-start.14 = (f32[128,128]{1,0:T(8,128)}, f32[128,128]{1,0:T(8,128)S(1)}, u32[]{:S(2)}, u32[]{:S(2)}) collective-permute-start(f32[128,128]{1,0:T(8,128)} %get-tuple-element.22), channel_id=1, source_target_pairs={{4,0},{8,4},{12,8},{16,12},{20,16},{24,20},{28,24},{5,1},{9,5},{13... | collective-permute-start | bytes 196616 | tf_op jit(solution)/shard_map/ppermute | solution.py:168
  148.6 7.3 %collective-permute-start.15 = (f32[128,128]{1,0:T(8,128)}, f32[128,128]{1,0:T(8,128)S(1)}, u32[]{:S(2)}, u32[]{:S(2)}) collective-permute-start(f32[128,128]{1,0:T(8,128)} %get-tuple-element.22), channel_id=1, source_target_pairs={{8,0},{12,4},{16,8},{20,12},{24,16},{28,20},{9,1},{13,5},{17,9},{2... | collective-permute-start | bytes 196616 | tf_op jit(solution)/shard_map/ppermute | solution.py:168
Sparse Core Ops, SparseCore 0:
  71.8 33.9 all-gather.1
where the time goes:
time: 164 us; the launch traced here: 163 us
  waiting for transfers between devices  84.3 us (51%)
  starting transfers between devices  33.4 us (20%)
  between operations  21 us (13%)
  matrix products  9.34 us (6%)
  Pallas kernels  6.26 us (4%)
  other arithmetic  5.94 us (4%)
  local copies, waits for them, and re-layouts  3.19 us (2%)
    ppermute x11, waiting for transfers between devices, from_behind(): return lax.ppermute(block, axis, route)  29.6 us
    ppermute x11, starting transfers between devices, from_behind(): return lax.ppermute(block, axis, route)  29 us
    ppermute x4, waiting for transfers between devices, spread(): got = lax.ppermute(block, axis, pairs)  27.5 us
    all_gather x1, waiting for transfers between devices, local(): gathered = lax.all_gather(compact, 'col', axis=0, tiled=True)  27.2 us
    dot_general x11, matrix products, product(): return jnp.dot(left, right, precision=lax.Precision.HIGH)  9.34 us
    pallas_call x1, Pallas kernels, fold(): pl.pallas_call(fold_kernel, out_shape=jax.ShapeDtypeStruct((SKEL, SKEL),...  6.26 us
    ppermute x4, starting transfers between devices, spread(): got = lax.ppermute(block, axis, pairs)  4.27 us
  transfers between devices with their start and end apart: 17, of which 7 were waited for; matrix products, arithmetic and copies ran while one was open for 9% of the time, Pallas kernels for 4%

commit v1 on v0

--- a/solution.py
+++ b/solution.py
@@ -11,6 +11,7 @@
 REACH = 2
 BLK = 128
 PANEL = 8
+CHUNKS = 2
 F32 = jnp.float32
 BF16 = jnp.bfloat16
 
@@ -133,49 +134,264 @@
     )(near_tile, basis)
 
 
-def fold_kernel(rotated_ref, out_ref, work):
-    load_block(work, rotated_ref[:SKEL, :SKEL])
+def exchange_kernel(
+    rows, cols, slot_ref, pick_ref, near_ref, skel_ref, combined_ref, factor_in,
+    factor_ref, merged_ref, diag_ref, strip_ref,
+    table, products, outgoing, incoming,
+    chain_send, chain_recv, row_send, row_recv, fact_send, fact_recv,
+    tile_send, tile_recv, pair_send, pair_recv, diag_send, diag_recv,
+):
+    row = lax.axis_index("row")
+    col = lax.axis_index("col")
+    entries = near_ref.shape[0]
+    order = combined_ref.shape[0]
+    red = order - SKEL
+    step = order // CHUNKS
+    reach_rows = 2 * ((REACH + 1) // 2) + 1
+    holder = row // 2
+    parity = row % 2
+    parent_reach = (REACH + 1) // 2
+
+    def remote(src, dst, send, recv, r, c):
+        return pltpu.make_async_remote_copy(
+            src_ref=src, dst_ref=dst, send_sem=send, recv_sem=recv,
+            device_id=(r, c), device_id_type=pl.DeviceIdType.MESH,
+        )
+
+    table[...] = jnp.zeros_like(table)
+    diag_ref[...] = jnp.zeros_like(diag_ref)
+    for lo in range(0, red - BLK, BLK):
+        factor_ref[lo : lo + BLK, lo + BLK :] = jnp.zeros((BLK, red - lo - BLK), F32)
+
+    barrier = pltpu.get_barrier_semaphore()
+    for d in range(-reach_rows, reach_rows + 1):
+        if d:
+            pl.semaphore_signal(
+                barrier, inc=1, device_id=(lax.rem(row + d + rows, rows), col),
+                device_id_type=pl.DeviceIdType.MESH,
+            )
+    for d in range(1, cols):
+        pl.semaphore_signal(
+            barrier, inc=1, device_id=(row, lax.rem(col + d, cols)),
+            device_id_type=pl.DeviceIdType.MESH,
+        )
+    pl.semaphore_wait(barrier, 2 * reach_rows + cols - 1)
+
+    @pl.when(col == 0)
+    def _():
+        table[REACH] = combined_ref[...]
+
+    def chunk(slot, k):
+        return table.at[slot, pl.ds(k * step, step), :]
+
+    def chain(k):
+        return remote(
+            chunk(REACH, k), chunk(REACH, k), chain_send.at[k], chain_recv.at[k], row,
+            lax.rem(col + 1, cols),
+        )
+
+    def to_row(d, k):
+        return remote(
+            chunk(REACH, k), chunk(REACH - d, k), row_send.at[d + REACH, k],
+            row_recv.at[REACH - d, k], lax.rem(row + d + rows, rows), col,
+        )
+
+    offsets = [d for d in range(-REACH, REACH + 1) if d]
+    for k in range(CHUNKS):
+        @pl.when(col > 0)
+        def _():
+            chain(k).wait_recv()
+
+        @pl.when(col < cols - 1)
+        def _():
+            chain(k).start()
+
+        for d in offsets:
+            @pl.when((row + d >= 0) & (row + d < rows))
+            def _():
+                to_row(d, k).start()
+
+    def strip(j):
+        return factor_ref.at[pl.ds(j * BLK, BLK), pl.ds(0, (j + 1) * BLK)]
+
+    def send_factor(d, j):
+        return remote(strip(j), strip(j), fact_send.at[d, j], fact_recv.at[j], row, d)
+
+    @pl.when(col == 0)
+    def _():
+        factor_ref[...] = factor_in[...]
+        for d in range(1, cols):
+            for j in range(red // BLK):
+                send_factor(d, j).start()
+
+    for e in range(entries):
+        products[e] = mm(skel_ref[...], near_ref[e], TN)
+
+    for k in range(CHUNKS):
+        for d in offsets:
+            @pl.when((row + d >= 0) & (row + d < rows))
+            def _():
+                to_row(-d, k).wait_recv()
+
+    tiles = [mm(products[e], table[slot_ref[e]], NN) for e in range(entries)]
+    zero = jnp.zeros((SKEL, SKEL), F32)
+    for t in range(2 * cols):
+        total = zero
+        for e in range(entries):
+            total = total + jnp.where(pick_ref[t * entries + e] > 0, tiles[e], zero)
+        outgoing[t // 2, :, (t % 2) * SKEL : (t % 2 + 1) * SKEL] = total
+
+    def send_tile(d):
+        other = lax.rem(col + d, cols)
+        return remote(
+            outgoing.at[other], incoming.at[d], tile_send.at[d], tile_recv.at[d], row, other
+        )
+
+    for d in range(1, cols):
+        send_tile(d).start()
+    total = outgoing[col]
+    for d in range(1, cols):
+        send_tile(d).wait_recv()
+        total = total + incoming[d]
+    strip_ref[...] = total
+    merged_ref[parity] = total
+
+    to_pair = remote(
+        strip_ref, merged_ref.at[parity], pair_send, pair_recv, row + 1 - 2 * parity, col
+    )
+    to_pair.start()
+
+    def to_diag(d):
+        return remote(
+            strip_ref, diag_ref.at[parity], diag_send.at[d + reach_rows],
+            diag_recv.at[parity], lax.rem(row + d + rows, rows), col,
+        )
+
+    def sends_diag(d):
+        other = row + d
+        near = ((other + 2 * parent_reach) // 2 >= col) & (other // 2 <= col + parent_reach)
+        return (holder == col) & (other >= 0) & (other < rows) & near
+
+    @pl.when(holder == col)
+    def _():
+        diag_ref[parity] = total
+
+    for d in range(-reach_rows, reach_rows + 1):
+        if d:
+            @pl.when(sends_diag(d))
+            def _():
+                to_diag(d).start()
+
+    remote(
+        strip_ref, merged_ref.at[1 - parity], pair_send, pair_recv, row + 1 - 2 * parity, col
+    ).wait_recv()
+    inside = (holder + parent_reach >= col) & (holder <= col + parent_reach)
+    for s in range(2):
+        @pl.when(inside & (row - 2 * col - s != 0))
+        def _():
+            remote(
+                strip_ref, diag_ref.at[s], diag_send.at[0], diag_recv.at[s],
+                row + 1 - 2 * parity, col,
+            ).wait_recv()
+
+    @pl.when(col > 0)
+    def _():
+        for j in range(red // BLK):
+            send_factor(0, j).wait_recv()
+
+    to_pair.wait_send()
+    for d in range(-reach_rows, reach_rows + 1):
+        if d:
+            @pl.when(sends_diag(d))
+            def _():
+                to_diag(d).wait_send()
+    for d in range(1, cols):
+        send_tile(d).wait_send()
+    for k in range(CHUNKS):
+        @pl.when(col < cols - 1)
+        def _():
+            chain(k).wait_send()
+
+        for d in offsets:
+            @pl.when((row + d >= 0) & (row + d < rows))
+            def _():
+                to_row(d, k).wait_send()
+
+    @pl.when(col == 0)
+    def _():
+        for d in range(1, cols):
+            for j in range(red // BLK):
+                send_factor(d, j).wait_send()
+
+
+def exchange(slots, picks, near, skel_basis, combined, factor):
+    rows, cols = lax.axis_size("row"), lax.axis_size("col")
+    order = combined.shape[0]
+    red = factor.shape[0]
+    entries = near.shape[0]
+    reach_rows = 2 * ((REACH + 1) // 2) + 1
+    spans = 2 * REACH + 1
+    vmem = pl.BlockSpec(memory_space=pltpu.VMEM)
+    smem = pl.BlockSpec(memory_space=pltpu.SMEM)
+    dma = pltpu.SemaphoreType.DMA
+    return pl.pallas_call(
+        functools.partial(exchange_kernel, rows, cols),
+        out_shape=(
+            jax.ShapeDtypeStruct((red, red), F32),
+            jax.ShapeDtypeStruct((2, SKEL, 2 * SKEL), F32),
+            jax.ShapeDtypeStruct((2, SKEL, 2 * SKEL), F32),
+            jax.ShapeDtypeStruct((SKEL, 2 * SKEL), F32),
+        ),
+        in_specs=[smem, smem, vmem, vmem, vmem, vmem],
+        out_specs=[vmem] * 4,
+        scratch_shapes=[
+            pltpu.VMEM((spans, order, SKEL), F32),
+            pltpu.VMEM((entries, SKEL, order), F32),
+            pltpu.VMEM((cols, SKEL, 2 * SKEL), F32),
+            pltpu.VMEM((cols, SKEL, 2 * SKEL), F32),
+            dma((CHUNKS,)), dma((CHUNKS,)),
+            dma((spans, CHUNKS)), dma((spans, CHUNKS)),
+            dma((cols, red // BLK)), dma((red // BLK,)),
+            dma((cols,)), dma((cols,)),
+            dma, dma,
+            dma((2 * reach_rows + 1,)), dma((2,)),
+        ],
+        compiler_params=pltpu.CompilerParams(
+            collective_id=0, has_side_effects=True, vmem_limit_bytes=40 * 1024 * 1024
+        ),
+        name="exchange",
+    )(slots, picks, near, skel_basis, combined, factor)
+
+
+def parent_kernel(merged_ref, diag_ref, row_basis, col_basis, out_ref, work):
+    basis = col_basis[...]
+    pivot_block = mm(basis, mm(diag_ref[...], basis, NN), TN)
+    rotated = mm(row_basis[:, SKEL:], mm(merged_ref[...], basis, NN), TN)
+    row = lax.broadcasted_iota(jnp.int32, (BLK, BLK), 0)
+    eye = jnp.where(row == lax.broadcasted_iota(jnp.int32, (BLK, BLK), 1), 1.0, 0.0)
+    inside = jnp.abs(lax.axis_index("row") // 2 - lax.axis_index("col")) <= (REACH + 1) // 2
+    load_block(work, jnp.where(inside, pivot_block[:SKEL, :SKEL], eye))
     chol_inv(work)
     inverse = work[:, BLK:]
-    out_ref[...] = mm(inverse, mm(inverse, rotated_ref[:SKEL, SKEL:], NN), TN)
-
-
-def fold(rotated):
+    folded = mm(inverse, mm(inverse, pivot_block[:SKEL, SKEL:], NN), TN)
+    out_ref[...] = rotated[:, SKEL:] - mm(rotated[:, :SKEL], folded, NN)
+
+
+def parent(merged, diag, row_basis, col_basis):
     return pl.pallas_call(
-        fold_kernel,
+        parent_kernel,
         out_shape=jax.ShapeDtypeStruct((SKEL, SKEL), F32),
-        in_specs=[pl.BlockSpec(memory_space=pltpu.VMEM)],
+        in_specs=[pl.BlockSpec(memory_space=pltpu.VMEM)] * 4,
         out_specs=pl.BlockSpec(memory_space=pltpu.VMEM),
         scratch_shapes=[pltpu.VMEM((BLK, 2 * BLK), F32)],
-        name="parent_pivot",
-    )(rotated)
-
-
-def spread(block, axis):
-    step = lax.axis_size(axis) // 2
-    index = lax.axis_index(axis)
-    while step >= 1:
-        pairs = [(i, i + step) for i in range(0, lax.axis_size(axis), 2 * step)]
-        got = lax.ppermute(block, axis, pairs)
-        block = jnp.where(index % (2 * step) == step, got, block)
-        step //= 2
-    return block
+        name="parent",
+    )(merged, diag, row_basis, col_basis)
 
 
 def from_behind(block, axis, distance):
     devices = range(lax.axis_size(axis))
     route = [(i - distance, i) for i in devices if i - distance in devices]
     return lax.ppermute(block, axis, route)
-
-
-def swapped(value, axis, distance):
-    mask = 2**distance
-    pairs = [(source, source ^ mask) for source in range(lax.axis_size(axis))]
-    return lax.ppermute(value, axis, pairs)
-
-
-def product(left, right):
-    return jnp.dot(left, right, precision=lax.Precision.HIGH)
 
 
 def local(near_blocks, leaf_bases, upper_bases, near_list):
@@ -189,6 +405,12 @@
     own_basis = leaf_bases[0]
     near_row = near_list[0]
     parent_reach = (REACH + 1) // 2
+    upper_basis = upper_bases[0]
+    pieces = []
+    for offset in range(-parent_reach, parent_reach + 1):
+        pieces.append(upper_basis if offset == 0 else from_behind(upper_basis, "col", -offset))
+    basis_slot = jnp.clip(holder - col_index + parent_reach, 0, 2 * parent_reach)
+    row_basis = lax.select_n(basis_slot, *pieces)
 
     def blank_pivot(near_tile, basis):
         return (
@@ -199,70 +421,22 @@
     factor, combined = lax.cond(
         col_index == 0, pivot, blank_pivot, near_blocks[0, 0], own_basis
     )
-    combined = spread(combined, "col")
-    factor = spread(factor, "col")
-    skel_basis_t = own_basis[:, red_count:].T
-    row_products = []
-    slot_list = []
-    for entry in range(entry_count):
-        row_products.append(product(skel_basis_t, near_blocks[0, entry]))
-        col_leaf = lax.dynamic_index_in_dim(
-            near_row, col_index * entry_count + entry, 0, keepdims=False
-        )
-        slot_list.append(col_leaf - row_index + REACH)
-    tile_list = []
-    combined_list = []
-    for offset in range(-REACH, REACH + 1):
-        if offset == 0:
-            combined_list.append(combined)
-        else:
-            combined_list.append(from_behind(combined, "row", -offset))
-    combined_table = jnp.stack(combined_list)
-    for entry in range(entry_count):
-        column_part = lax.dynamic_index_in_dim(combined_table, slot_list[entry], 0, keepdims=False)
-        tile_list.append(product(row_products[entry], column_part))
-    compact = jnp.stack(tile_list)
-    gathered = lax.all_gather(compact, "col", axis=0, tiled=True)
-    strips = []
-    for column_slot in range(2):
-        target_leaf = col_index * 2 + column_slot
-        matches = near_row == target_leaf
-        first_match = jnp.argmax(matches)
-        picked = lax.dynamic_index_in_dim(gathered, first_match, 0, keepdims=False)
-        strips.append(jnp.where(jnp.any(matches), picked, jnp.zeros_like(picked)))
-    skeleton_strip = jnp.concatenate(strips, axis=1)
-    partner = swapped(skeleton_strip, "row", 0)
-    merged = jnp.where(
-        row_slot == 0,
-        jnp.concatenate([skeleton_strip, partner], axis=0),
-        jnp.concatenate([partner, skeleton_strip], axis=0),
-    )
-    upper_basis = upper_bases[0]
-    basis_pieces = []
-    for offset in range(-parent_reach, parent_reach + 1):
-        if offset == 0:
-            basis_pieces.append(upper_basis)
-        else:
-            basis_pieces.append(from_behind(upper_basis, "col", -offset))
-    parent_table = jnp.stack(basis_pieces)
-    basis_slot = jnp.clip(holder - col_index + parent_reach, 0, 2 * parent_reach)
-    parent_basis = lax.dynamic_index_in_dim(parent_table, basis_slot, 0, keepdims=False)
-    parent_rotated = product(parent_basis.T, product(merged, upper_basis))
-    folded = lax.cond(
-        row_index == col_index * 2, fold, lambda block: jnp.zeros((SKEL, SKEL), F32), parent_rotated
-    )
-    pieces = []
-    for offset in range(-2 * parent_reach - 1, 2 * parent_reach + 1):
-        pieces.append(folded if offset == 0 else from_behind(folded, "row", -offset))
-    pivot_slot = jnp.clip(2 * col_index - row_index + 2 * parent_reach + 1, 0, 4 * parent_reach + 1)
-    chosen = lax.dynamic_index_in_dim(jnp.stack(pieces), pivot_slot, 0, keepdims=False)
-    in_window = jnp.abs(holder - col_index) <= parent_reach
-    chosen = jnp.where(in_window, chosen, jnp.zeros_like(chosen))
-    low_rows = lax.dynamic_slice_in_dim(
-        parent_rotated, SKEL + row_slot * (SKEL // 2), SKEL // 2, 0
-    )
-    upper_half = low_rows[:, SKEL:] - product(low_rows[:, :SKEL], chosen)
-    return (factor, skeleton_strip, upper_half)
+    mine = lax.dynamic_slice_in_dim(near_row, col_index * entry_count, entry_count, 0)
+    slots = jnp.clip(mine - row_index + REACH, 0, 2 * REACH)
+    leaves = jnp.arange(2 * lax.axis_size("col"), dtype=jnp.int32)
+    matches = near_row[None, :] == leaves[:, None]
+    first = jnp.argmax(matches, axis=1).astype(jnp.int32)
+    places = col_index * entry_count + jnp.arange(entry_count, dtype=jnp.int32)
+    picks = jnp.any(matches, axis=1)[:, None] & (first[:, None] == places[None, :])
+    factor, merged, diag, strip = exchange(
+        slots, picks.astype(jnp.int32).reshape(-1), near_blocks[0], own_basis[:, red_count:],
+        combined, factor,
+    )
+    upper_full = parent(
+        merged.reshape(2 * SKEL, 2 * SKEL), diag.reshape(2 * SKEL, 2 * SKEL), row_basis, upper_basis
+    )
+    upper_half = lax.dynamic_slice_in_dim(upper_full, row_slot * (SKEL // 2), SKEL // 2, 0)
+    return (factor, strip, upper_half)
 
 
 def solution(mesh):

time: 164 us -> 100 us (0.61)
  the two profiles are of different devices: /device:TPU:10 before, /device:TPU:13 now
where the time goes in v1:
time: 100 us; the launch traced here: 99.8 us
  Pallas kernels  85.4 us (85%)
  local copies, waits for them, and re-layouts  5.36 us (5%)
  starting transfers between devices  5.3 us (5%)
  other arithmetic  2.97 us (3%)
    pallas_call x1, Pallas kernels, exchange(): pl.pallas_call(functools.partial(exchange_kernel, rows, cols), out_shape=...  77.2 us
    pallas_call x1, Pallas kernels, parent(): pl.pallas_call(parent_kernel, out_shape=jax.ShapeDtypeStruct((SKEL, SKEL)...  8.27 us
    ppermute x2, starting transfers between devices, from_behind(): return lax.ppermute(block, axis, route)  5.3 us
    unnamed x10, local copies, waits for them, and re-layouts  2.87 us
  transfers between devices with their start and end apart: 2, of which 0 were waited for; matrix products, arithmetic and copies ran while one was open for 3% of the time, Pallas kernels for 77%

profile of v1, /device:TPU:13, one launch (start us, length us, event | category | flops | bytes accessed | tf_op | source)
XLA Modules:
  0.0 99.8 jit_solution(13746159622544947818)
XLA Ops:
  0.6 0.0 copy-start.3
  0.6 3.2 %collective-permute-start = (f32[256,256]{1,0:T(8,128)}, f32[256,256]{1,0:T(8,128)S(1)}, u32[]{:S(2)}, u32[]{:S(2)}) collective-permute-start(f32[256,256]{1,0:T(8,128)} %bitcast.16), channel_id=1, source_target_pairs={{0,1},{1,2},{2,3},{4,5},{5,6},{6,7},{8,9},{9,10},{10,11},{12,13},{... | collective-permute-start | bytes 786440 | tf_op jit(solution)/shard_map/ppermute | solution.py:394
  3.9 2.1 %collective-permute-start.1 = (f32[256,256]{1,0:T(8,128)}, f32[256,256]{1,0:T(8,128)S(1)}, u32[]{:S(2)}, u32[]{:S(2)}) collective-permute-start(f32[256,256]{1,0:T(8,128)} %bitcast.17), channel_id=1, source_target_pairs={{1,0},{2,1},{3,2},{5,4},{6,5},{7,6},{9,8},{10,9},{11,10},{13,12},{... | collective-permute-start | bytes 786440 | tf_op jit(solution)/shard_map/ppermute | solution.py:394
  6.0 1.3 %iota_reduce_fusion = (pred[8]{0:T(512)(128)(4,1)}, s32[8]{0:T(128)S(1)}) fusion(s32[16]{0:T(128)} %bitcast.19), kind=kLoop, calls=%fused_computation.2 | loop fusion | flops 968 | bytes 104 | tf_op jit(solution)/shard_map/local/reduce | solution.py:428
  7.2 0.8 fusion
  8.1 0.1 and_convert_fusion
  8.1 0.1 reshape.36.pick_ref
  8.2 1.0 slice.8.skel_ref
  9.2 0.0 copy-start.2
  9.2 0.1 conditional.1
  9.3 0.0 copy-done.3
  9.3 0.1 clamp_bitcast_fusion.slot_ref
  9.4 77.2 %exchange.1 = (f32[384,384]{1,0:T(8,128)S(1)}, f32[2,128,256]{2,1,0:T(8,128)S(1)}, f32[2,128,256]{2,1,0:T(8,128)S(1)}, f32[128,256]{1,0:T(8,128)S(1)}) custom-call(s32[4]{0:T(128)S(1)} %clamp_bitcast_fusion.slot_ref, s32[32]{0:T(128)S(1)} %reshape.36.pick_ref, f32[4,512,512]{2,1,0:T(8,128)} %bitcast.13, f32[512,128]{1,0:T(8,128)S(1)} %slice.8.skel_ref, ...), custom_call_target="tpu_custom_call" | custom-call | tf_op jit(solution)/shard_map/exchange/pallas_call | solution.py:337
  86.6 0.0 copy-start
  86.6 0.7 copy-done
  87.3 0.0 copy-start.1
  87.3 0.7 copy-done.1
  88.0 0.0 collective-permute-done
  88.0 0.0 collective-permute-done.1
  88.0 0.0 copy-done.2
  88.0 0.8 select_select_fusion.row_basis
  88.7 8.3 %parent.1 = f32[128,128]{1,0:T(8,128)} custom-call(f32[256,256]{1,0:T(8,128)} %bitcast.11, f32[256,256]{1,0:T(8,128)} %bitcast.12, f32[256,256]{1,0:T(8,128)} %select_select_fusion.row_basis, f32[256,256]{1,0:T(8,128)} %bitcast.18), custom_call_target="tpu_custom_call" | custom-call | tf_op jit(solution)/shard_map/parent/pallas_call | solution.py:381
  97.0 1.4 %constant_dynamic-slice_fusion = f32[64,128]{1,0:T(8,128)} fusion(f32[128,128]{1,0:T(8,128)} %parent.1, s32[]{:T(128)S(6)} %select_n.48), kind=kLoop, calls=%fused_computation.8 | loop fusion | bytes 65540 | tf_op jit(solution)/shard_map/dynamic_slice | solution.py:438
  98.4 0.8 copy.13
  99.2 0.7 copy.14
  (3 shorter events, 0.1 us)
Async XLA Ops:
  0.6 8.7 %copy-start.3 = (s32[1,16]{1,0:T(1,128)S(1)}, s32[1,16]{1,0:T(1,128)}, u32[]{:S(2)}) copy-start(s32[1,16]{1,0:T(1,128)} %param.9) | copy-start | bytes 196
  0.6 87.3 %collective-permute-start = (f32[256,256]{1,0:T(8,128)}, f32[256,256]{1,0:T(8,128)S(1)}, u32[]{:S(2)}, u32[]{:S(2)}) collective-permute-start(f32[256,256]{1,0:T(8,128)} %bitcast.16), channel_id=1, source_target_pairs={{0,1},{1,2},{2,3},{4,5},{5,6},{6,7},{8,9},{9,10},{10,11},{12,13},{... | collective-permute-start | bytes 786440 | tf_op jit(solution)/shard_map/ppermute | solution.py:394
  3.9 84.1 %collective-permute-start.1 = (f32[256,256]{1,0:T(8,128)}, f32[256,256]{1,0:T(8,128)S(1)}, u32[]{:S(2)}, u32[]{:S(2)}) collective-permute-start(f32[256,256]{1,0:T(8,128)} %bitcast.17), channel_id=1, source_target_pairs={{1,0},{2,1},{3,2},{5,4},{6,5},{7,6},{9,8},{10,9},{11,10},{13,12},{... | collective-permute-start | bytes 786440 | tf_op jit(solution)/shard_map/ppermute | solution.py:394
  9.2 78.8 %copy-start.2 = (f32[1,256,256]{2,1,0:T(8,128)S(1)}, f32[1,256,256]{2,1,0:T(8,128)}, u32[]{:S(2)}) copy-start(f32[1,256,256]{2,1,0:T(8,128)} %param.8) | copy-start | bytes 786436
  86.6 0.7 copy-start
  87.3 0.7 copy-start.1

commit v2 on v1

--- a/solution.py
+++ b/solution.py
@@ -11,7 +11,7 @@
 REACH = 2
 BLK = 128
 PANEL = 8
-CHUNKS = 2
+CHUNKS = 4
 F32 = jnp.float32
 BF16 = jnp.bfloat16
 
@@ -87,7 +87,7 @@
     order = basis_ref.shape[0]
     red = order - SKEL
     count = red // BLK
-    rotated = mm(basis_ref[:, :red], mm(near_ref[...], basis_ref[...], NN), TN)
+    rotated = mm(basis_ref[:, :red], mm(near_ref[0], basis_ref[...], NN), TN)
     square = rotated[:, :red]
     mat[:, :red] = (square + square.T) * 0.5
     mat[:, red:] = rotated[:, red:]
@@ -117,7 +117,7 @@
     )
 
 
-def pivot(near_tile, basis):
+def pivot(near, basis):
     order = basis.shape[0]
     red = order - SKEL
     return pl.pallas_call(
@@ -126,24 +126,32 @@
             jax.ShapeDtypeStruct((red, red), F32),
             jax.ShapeDtypeStruct((order, SKEL), F32),
         ),
-        in_specs=[pl.BlockSpec(memory_space=pltpu.VMEM)] * 2,
-        out_specs=[pl.BlockSpec(memory_space=pltpu.VMEM)] * 2,
+        grid=(1,),
+        in_specs=[
+            pl.BlockSpec((1, order, order), lambda i: (0, 0, 0)),
+            pl.BlockSpec((order, order), lambda i: (0, 0)),
+        ],
+        out_specs=[
+            pl.BlockSpec((red, red), lambda i: (0, 0)),
+            pl.BlockSpec((order, SKEL), lambda i: (0, 0)),
+        ],
         scratch_shapes=[pltpu.VMEM((red, order), F32), pltpu.VMEM((BLK, 2 * BLK), F32)],
         compiler_params=pltpu.CompilerParams(vmem_limit_bytes=32 * 1024 * 1024),
         name="leaf_pivot",
-    )(near_tile, basis)
+    )(near, basis)
 
 
 def exchange_kernel(
-    rows, cols, slot_ref, pick_ref, near_ref, skel_ref, combined_ref, factor_in,
-    factor_ref, merged_ref, diag_ref, strip_ref,
-    table, products, outgoing, incoming,
+    rows, cols, list_ref, near_hbm, basis_ref, upper_ref, combined_ref, factor_in,
+    factor_ref, merged_ref, diag_ref, strip_ref, row_basis_ref,
+    near_ref, upper_half, table, products, outgoing, incoming,
     chain_send, chain_recv, row_send, row_recv, fact_send, fact_recv,
     tile_send, tile_recv, pair_send, pair_recv, diag_send, diag_recv,
+    near_sem, basis_send, basis_recv,
 ):
     row = lax.axis_index("row")
     col = lax.axis_index("col")
-    entries = near_ref.shape[0]
+    entries = near_hbm.shape[0]
     order = combined_ref.shape[0]
     red = order - SKEL
     step = order // CHUNKS
@@ -158,6 +166,21 @@
             device_id=(r, c), device_id_type=pl.DeviceIdType.MESH,
         )
 
+    loads = [
+        pltpu.make_async_copy(near_hbm.at[e], near_ref.at[e], near_sem.at[e])
+        for e in range(entries)
+    ]
+    for load in loads:
+        load.start()
+
+    def row_products():
+        skel = basis_ref[:, red:]
+        for e in range(entries):
+            loads[e].wait()
+            products[e] = mm(skel, near_ref[e], TN)
+
+    upper_half[...] = upper_ref[:, SKEL:]
+    row_basis_ref[...] = jnp.where(holder == col, upper_ref[:, SKEL:], 0.0)
     table[...] = jnp.zeros_like(table)
     diag_ref[...] = jnp.zeros_like(diag_ref)
     for lo in range(0, red - BLK, BLK):
@@ -175,6 +198,11 @@
             barrier, inc=1, device_id=(row, lax.rem(col + d, cols)),
             device_id_type=pl.DeviceIdType.MESH,
         )
+
+    @pl.when(col > 0)
+    def _():
+        row_products()
+
     pl.semaphore_wait(barrier, 2 * reach_rows + cols - 1)
 
     @pl.when(col == 0)
@@ -214,18 +242,41 @@
     def strip(j):
         return factor_ref.at[pl.ds(j * BLK, BLK), pl.ds(0, (j + 1) * BLK)]
 
-    def send_factor(d, j):
-        return remote(strip(j), strip(j), fact_send.at[d, j], fact_recv.at[j], row, d)
+    def send_factor(j):
+        return remote(
+            strip(j), strip(j), fact_send.at[j], fact_recv.at[j], row, lax.rem(col + 1, cols)
+        )
+
+    def send_basis(d):
+        return remote(
+            upper_half, row_basis_ref, basis_send.at[d + parent_reach], basis_recv, row,
+            lax.rem(col + d + cols, cols),
+        )
+
+    def sends_basis(d):
+        return (holder == col) & (col + d >= 0) & (col + d < cols)
 
     @pl.when(col == 0)
     def _():
         factor_ref[...] = factor_in[...]
-        for d in range(1, cols):
-            for j in range(red // BLK):
-                send_factor(d, j).start()
-
-    for e in range(entries):
-        products[e] = mm(skel_ref[...], near_ref[e], TN)
+        for j in range(red // BLK):
+            send_factor(j).start()
+        row_products()
+
+    for d in range(-parent_reach, parent_reach + 1):
+        if d:
+            @pl.when(sends_basis(d))
+            def _():
+                send_basis(d).start()
+
+    def forward_factor():
+        for j in range(red // BLK):
+            send_factor(j).wait_recv()
+            send_factor(j).start()
+
+    @pl.when((col == 1) & (col < cols - 1))
+    def _():
+        forward_factor()
 
     for k in range(CHUNKS):
         for d in offsets:
@@ -233,12 +284,24 @@
             def _():
                 to_row(-d, k).wait_recv()
 
-    tiles = [mm(products[e], table[slot_ref[e]], NN) for e in range(entries)]
+    own = [list_ref[0, col * entries + e] for e in range(entries)]
+    leads = []
+    for e in range(entries):
+        seen = jnp.int32(0)
+        for k in range(list_ref.shape[1]):
+            same = (list_ref[0, k] == own[e]).astype(jnp.int32)
+            before = (k < col * entries + e).astype(jnp.int32)
+            seen = jnp.maximum(seen, same * before)
+        leads.append(jnp.where(seen == 0, own[e], -1))
+    tiles = []
+    for e in range(entries):
+        slot = jnp.clip(own[e] - row + REACH, 0, 2 * REACH)
+        tiles.append(mm(products[e], table[slot], NN))
     zero = jnp.zeros((SKEL, SKEL), F32)
     for t in range(2 * cols):
         total = zero
         for e in range(entries):
-            total = total + jnp.where(pick_ref[t * entries + e] > 0, tiles[e], zero)
+            total = total + jnp.where(leads[e] == t, tiles[e], zero)
         outgoing[t // 2, :, (t % 2) * SKEL : (t % 2 + 1) * SKEL] = total
 
     def send_tile(d):
@@ -249,6 +312,11 @@
 
     for d in range(1, cols):
         send_tile(d).start()
+
+    @pl.when((col > 1) & (col < cols - 1))
+    def _():
+        forward_factor()
+
     total = outgoing[col]
     for d in range(1, cols):
         send_tile(d).wait_recv()
@@ -294,10 +362,20 @@
                 row + 1 - 2 * parity, col,
             ).wait_recv()
 
-    @pl.when(col > 0)
+    @pl.when((col == cols - 1) & (col > 0))
     def _():
         for j in range(red // BLK):
-            send_factor(0, j).wait_recv()
+            send_factor(j).wait_recv()
+
+    for d in range(-parent_reach, parent_reach + 1):
+        if d:
+            @pl.when(holder + d == col)
+            def _():
+                send_basis(d).wait_recv()
+
+            @pl.when(sends_basis(d))
+            def _():
+                send_basis(d).wait_send()
 
     to_pair.wait_send()
     for d in range(-reach_rows, reach_rows + 1):
@@ -317,14 +395,13 @@
             def _():
                 to_row(d, k).wait_send()
 
-    @pl.when(col == 0)
-    def _():
-        for d in range(1, cols):
-            for j in range(red // BLK):
-                send_factor(d, j).wait_send()
-
-
-def exchange(slots, picks, near, skel_basis, combined, factor):
+    @pl.when(col < cols - 1)
+    def _():
+        for j in range(red // BLK):
+            send_factor(j).wait_send()
+
+
+def exchange(near_row, near, basis, upper_basis, combined, factor):
     rows, cols = lax.axis_size("row"), lax.axis_size("col")
     order = combined.shape[0]
     red = factor.shape[0]
@@ -341,32 +418,36 @@
             jax.ShapeDtypeStruct((2, SKEL, 2 * SKEL), F32),
             jax.ShapeDtypeStruct((2, SKEL, 2 * SKEL), F32),
             jax.ShapeDtypeStruct((SKEL, 2 * SKEL), F32),
+            jax.ShapeDtypeStruct((2 * SKEL, SKEL), F32),
         ),
-        in_specs=[smem, smem, vmem, vmem, vmem, vmem],
-        out_specs=[vmem] * 4,
+        in_specs=[smem, pl.BlockSpec(memory_space=pl.ANY), vmem, vmem, vmem, vmem],
+        out_specs=[vmem] * 5,
         scratch_shapes=[
+            pltpu.VMEM(near.shape, F32),
+            pltpu.VMEM((2 * SKEL, SKEL), F32),
             pltpu.VMEM((spans, order, SKEL), F32),
             pltpu.VMEM((entries, SKEL, order), F32),
             pltpu.VMEM((cols, SKEL, 2 * SKEL), F32),
             pltpu.VMEM((cols, SKEL, 2 * SKEL), F32),
             dma((CHUNKS,)), dma((CHUNKS,)),
             dma((spans, CHUNKS)), dma((spans, CHUNKS)),
-            dma((cols, red // BLK)), dma((red // BLK,)),
+            dma((red // BLK,)), dma((red // BLK,)),
             dma((cols,)), dma((cols,)),
             dma, dma,
             dma((2 * reach_rows + 1,)), dma((2,)),
+            dma((entries,)), dma((2 * ((REACH + 1) // 2) + 1,)), dma,
         ],
         compiler_params=pltpu.CompilerParams(
             collective_id=0, has_side_effects=True, vmem_limit_bytes=40 * 1024 * 1024
         ),
         name="exchange",
-    )(slots, picks, near, skel_basis, combined, factor)
+    )(near_row, near, basis, upper_basis, combined, factor)
 
 
 def parent_kernel(merged_ref, diag_ref, row_basis, col_basis, out_ref, work):
     basis = col_basis[...]
     pivot_block = mm(basis, mm(diag_ref[...], basis, NN), TN)
-    rotated = mm(row_basis[:, SKEL:], mm(merged_ref[...], basis, NN), TN)
+    rotated = mm(row_basis[...], mm(merged_ref[...], basis, NN), TN)
     row = lax.broadcasted_iota(jnp.int32, (BLK, BLK), 0)
     eye = jnp.where(row == lax.broadcasted_iota(jnp.int32, (BLK, BLK), 1), 1.0, 0.0)
     inside = jnp.abs(lax.axis_index("row") // 2 - lax.axis_index("col")) <= (REACH + 1) // 2
@@ -374,13 +455,15 @@
     chol_inv(work)
     inverse = work[:, BLK:]
     folded = mm(inverse, mm(inverse, pivot_block[:SKEL, SKEL:], NN), TN)
-    out_ref[...] = rotated[:, SKEL:] - mm(rotated[:, :SKEL], folded, NN)
+    full = rotated[:, SKEL:] - mm(rotated[:, :SKEL], folded, NN)
+    half = SKEL // 2
+    out_ref[...] = jnp.where(lax.axis_index("row") % 2 == 0, full[:half], full[half:])
 
 
 def parent(merged, diag, row_basis, col_basis):
     return pl.pallas_call(
         parent_kernel,
-        out_shape=jax.ShapeDtypeStruct((SKEL, SKEL), F32),
+        out_shape=jax.ShapeDtypeStruct((SKEL // 2, SKEL), F32),
         in_specs=[pl.BlockSpec(memory_space=pltpu.VMEM)] * 4,
         out_specs=pl.BlockSpec(memory_space=pltpu.VMEM),
         scratch_shapes=[pltpu.VMEM((BLK, 2 * BLK), F32)],
@@ -388,54 +471,21 @@
     )(merged, diag, row_basis, col_basis)
 
 
-def from_behind(block, axis, distance):
-    devices = range(lax.axis_size(axis))
-    route = [(i - distance, i) for i in devices if i - distance in devices]
-    return lax.ppermute(block, axis, route)
-
-
 def local(near_blocks, leaf_bases, upper_bases, near_list):
-    leaf_order = leaf_bases.shape[1]
-    red_count = leaf_order - SKEL
-    entry_count = near_blocks.shape[1]
-    row_index = lax.axis_index("row")
-    col_index = lax.axis_index("col")
-    row_slot = row_index % 2
-    holder = row_index // 2
-    own_basis = leaf_bases[0]
-    near_row = near_list[0]
-    parent_reach = (REACH + 1) // 2
-    upper_basis = upper_bases[0]
-    pieces = []
-    for offset in range(-parent_reach, parent_reach + 1):
-        pieces.append(upper_basis if offset == 0 else from_behind(upper_basis, "col", -offset))
-    basis_slot = jnp.clip(holder - col_index + parent_reach, 0, 2 * parent_reach)
-    row_basis = lax.select_n(basis_slot, *pieces)
-
-    def blank_pivot(near_tile, basis):
-        return (
-            jnp.zeros((red_count, red_count), F32),
-            jnp.zeros((leaf_order, SKEL), F32),
-        )
-
-    factor, combined = lax.cond(
-        col_index == 0, pivot, blank_pivot, near_blocks[0, 0], own_basis
+    order = leaf_bases.shape[1]
+    red = order - SKEL
+    near, basis, upper_basis = near_blocks[0], leaf_bases[0], upper_bases[0]
+
+    def blank_pivot(near, basis):
+        return jnp.zeros((red, red), F32), jnp.zeros((order, SKEL), F32)
+
+    factor, combined = lax.cond(lax.axis_index("col") == 0, pivot, blank_pivot, near, basis)
+    factor, merged, diag, strip, row_basis = exchange(
+        near_list, near, basis, upper_basis, combined, factor
     )
-    mine = lax.dynamic_slice_in_dim(near_row, col_index * entry_count, entry_count, 0)
-    slots = jnp.clip(mine - row_index + REACH, 0, 2 * REACH)
-    leaves = jnp.arange(2 * lax.axis_size("col"), dtype=jnp.int32)
-    matches = near_row[None, :] == leaves[:, None]
-    first = jnp.argmax(matches, axis=1).astype(jnp.int32)
-    places = col_index * entry_count + jnp.arange(entry_count, dtype=jnp.int32)
-    picks = jnp.any(matches, axis=1)[:, None] & (first[:, None] == places[None, :])
-    factor, merged, diag, strip = exchange(
-        slots, picks.astype(jnp.int32).reshape(-1), near_blocks[0], own_basis[:, red_count:],
-        combined, factor,
-    )
-    upper_full = parent(
+    upper_half = parent(
         merged.reshape(2 * SKEL, 2 * SKEL), diag.reshape(2 * SKEL, 2 * SKEL), row_basis, upper_basis
     )
-    upper_half = lax.dynamic_slice_in_dim(upper_full, row_slot * (SKEL // 2), SKEL // 2, 0)
     return (factor, strip, upper_half)
 
 

time: 100 us -> 89.1 us (0.89)
  starting transfers between devices: 5.3 us -> 0 us
  other arithmetic: 2.97 us -> 0 us
  Pallas kernels: 85.4 us -> 83.7 us
    ppermute x2 -> x0, starting transfers between devices: 5.3 us -> none  [from_behind(): return lax.ppermute(block, axis, route)]
    pallas_call x1, Pallas kernels: 77.2 us -> 75.5 us  [exchange(): pl.pallas_call(functools.partial(exchange_kernel, rows, cols), out_shape=...]
    unnamed x10 -> x12, local copies, waits for them, and re-layouts: 2.87 us -> 4.36 us
    dynamic_slice x1 -> x0, local copies, waits for them, and re-layouts: 1.37 us -> none  [local(): lax.dynamic_slice_in_dim(upper_full, row_slot * (SKEL // 2), SKEL // 2, 0)]
    another operation x1 -> x0, other arithmetic: 1.29 us -> none  [local(): first = jnp.argmax(matches, axis=1).astype(jnp.int32)]
  transfers between devices with their start and end apart: 2 -> 0, of which waited for: 0 -> 0; matrix products, arithmetic and copies ran while one was open for 3% -> 0% of each run, Pallas kernels for 77% -> 0%
where the time goes in v2:
time: 89.1 us; the launch traced here: 88.9 us
  Pallas kernels  83.7 us (94%)
  local copies, waits for them, and re-layouts  4.42 us (5%)
    pallas_call x1, Pallas kernels, exchange(): pl.pallas_call(functools.partial(exchange_kernel, rows, cols), out_shape=...  75.5 us
    pallas_call x1, Pallas kernels, parent(): pl.pallas_call(parent_kernel, out_shape=jax.ShapeDtypeStruct((SKEL // 2,...  8.22 us
    unnamed x12, local copies, waits for them, and re-layouts  4.36 us

profile of v2, /device:TPU:13, one launch (start us, length us, event | category | flops | bytes accessed | tf_op | source)
XLA Modules:
  0.0 88.9 jit_solution(10758194303239710042)
XLA Ops:
  0.6 0.0 copy-start.4
  0.6 0.0 copy-start
  0.7 0.1 conditional.1
  0.8 0.5 copy-done.4
  1.3 0.3 copy-done
  1.6 75.5 %exchange.1 = (f32[384,384]{1,0:T(8,128)S(1)}, f32[2,128,256]{2,1,0:T(8,128)S(1)}, f32[2,128,256]{2,1,0:T(8,128)S(1)}, f32[128,256]{1,0:T(8,128)S(1)}, f32[256,128]{1,0:T(8,128)S(1)}) custom-call(s32[1,16]{1,0:T(1,128)S(1)} %copy-done.4, f32[4,512,512]{2,1,0:T(8,128)} %bitcast.10, f32[512,512]{1,0:T(8,128)} %bitcast.12, f32[256,256]{1,0:T(8,128)S(1)} %bitcast.6, ...), custom_call_target="tpu_custom_call" | custom-call | tf_op jit(solution)/shard_map/exchange/pallas_call | solution.py:414
  77.1 0.0 copy-start.1
  77.1 0.7 copy-done.1
  77.8 0.0 copy-start.2
  77.8 0.7 copy-done.2
  78.5 0.0 copy-start.3
  78.5 0.7 copy-done.3
  79.2 8.2 %parent.1 = f32[64,128]{1,0:T(8,128)} custom-call(f32[256,256]{1,0:T(8,128)} %bitcast.7, f32[256,256]{1,0:T(8,128)} %bitcast.8, f32[256,128]{1,0:T(8,128)} %copy-done.3, f32[256,256]{1,0:T(8,128)} %bitcast.5), custom_call_target="tpu_custom_call" | custom-call | tf_op jit(solution)/shard_map/parent/pallas_call | solution.py:464
  87.4 0.8 copy.13
  88.2 0.7 copy.14
  (2 shorter events, 0.1 us)
Async XLA Ops:
  0.6 0.7 copy-start.4
  0.6 1.0 %copy-start = (f32[1,256,256]{2,1,0:T(8,128)S(1)}, f32[1,256,256]{2,1,0:T(8,128)}, u32[]{:S(2)}) copy-start(f32[1,256,256]{2,1,0:T(8,128)} %param.8) | copy-start | bytes 786436
  77.1 0.7 copy-start.1
  77.8 0.7 copy-start.2
  78.5 0.7 copy-start.3

commit v3 on v2

--- a/solution.py
+++ b/solution.py
@@ -225,6 +225,24 @@
         )
 
     offsets = [d for d in range(-REACH, REACH + 1) if d]
+    toward = 1 - 2 * parity
+
+    def valid(d):
+        return (row + d >= 0) & (row + d < rows)
+
+    def direct(d):
+        return valid(d) & ((d % 2 == 0) | (toward == d))
+
+    def relay(k):
+        return remote(
+            chunk(REACH + 2 * toward, k), chunk(REACH + toward, k),
+            row_send.at[REACH - toward, k], row_recv.at[REACH + toward, k],
+            row + toward, col,
+        )
+
+    def relays():
+        return (row + 2 * toward >= 0) & (row + 2 * toward < rows)
+
     for k in range(CHUNKS):
         @pl.when(col > 0)
         def _():
@@ -235,7 +253,7 @@
             chain(k).start()
 
         for d in offsets:
-            @pl.when((row + d >= 0) & (row + d < rows))
+            @pl.when(direct(d))
             def _():
                 to_row(d, k).start()
 
@@ -279,8 +297,19 @@
         forward_factor()
 
     for k in range(CHUNKS):
+        @pl.when(relays())
+        def _():
+            remote(
+                chunk(REACH, k), chunk(REACH + 2 * toward, k), row_send.at[0, k],
+                row_recv.at[REACH + 2 * toward, k], row + toward, col,
+            ).wait_recv()
+            relay(k).start()
+
+    for k in range(CHUNKS):
         for d in offsets:
-            @pl.when((row + d >= 0) & (row + d < rows))
+            waiting = valid(d) if d % 2 else valid(d) & (2 * toward != d)
+
+            @pl.when(waiting)
             def _():
                 to_row(-d, k).wait_recv()
 
@@ -338,29 +367,35 @@
     def sends_diag(d):
         other = row + d
         near = ((other + 2 * parent_reach) // 2 >= col) & (other // 2 <= col + parent_reach)
-        return (holder == col) & (other >= 0) & (other < rows) & near
+        return (holder == col) & valid(d) & near & ((d % 2 == 0) | (toward == d))
 
     @pl.when(holder == col)
     def _():
         diag_ref[parity] = total
 
-    for d in range(-reach_rows, reach_rows + 1):
-        if d:
-            @pl.when(sends_diag(d))
-            def _():
-                to_diag(d).start()
+    for d in (-2, -1, 1, 2):
+        @pl.when(sends_diag(d))
+        def _():
+            to_diag(d).start()
 
     remote(
         strip_ref, merged_ref.at[1 - parity], pair_send, pair_recv, row + 1 - 2 * parity, col
     ).wait_recv()
     inside = (holder + parent_reach >= col) & (holder <= col + parent_reach)
-    for s in range(2):
-        @pl.when(inside & (row - 2 * col - s != 0))
-        def _():
-            remote(
-                strip_ref, diag_ref.at[s], diag_send.at[0], diag_recv.at[s],
-                row + 1 - 2 * parity, col,
-            ).wait_recv()
+
+    def from_diag(s):
+        return remote(
+            diag_ref.at[s], diag_ref.at[s], diag_send.at[0], diag_recv.at[s], row + toward, col
+        )
+
+    @pl.when(inside & (holder != col))
+    def _():
+        from_diag(parity).wait_recv()
+        from_diag(parity).start()
+
+    @pl.when(inside)
+    def _():
+        from_diag(1 - parity).wait_recv()
 
     @pl.when((col == cols - 1) & (col > 0))
     def _():
@@ -377,12 +412,15 @@
             def _():
                 send_basis(d).wait_send()
 
+    @pl.when(inside & (holder != col))
+    def _():
+        from_diag(parity).wait_send()
+
     to_pair.wait_send()
-    for d in range(-reach_rows, reach_rows + 1):
-        if d:
-            @pl.when(sends_diag(d))
-            def _():
-                to_diag(d).wait_send()
+    for d in (-2, -1, 1, 2):
+        @pl.when(sends_diag(d))
+        def _():
+            to_diag(d).wait_send()
     for d in range(1, cols):
         send_tile(d).wait_send()
     for k in range(CHUNKS):
@@ -391,9 +429,13 @@
             chain(k).wait_send()
 
         for d in offsets:
-            @pl.when((row + d >= 0) & (row + d < rows))
+            @pl.when(direct(d))
             def _():
                 to_row(d, k).wait_send()
+
+        @pl.when(relays())
+        def _():
+            relay(k).wait_send()
 
     @pl.when(col < cols - 1)
     def _():

time: 89.1 us -> 80.6 us (0.905)
  Pallas kernels: 83.7 us -> 75.3 us
    pallas_call x1, Pallas kernels: 75.5 us -> 67.1 us  [exchange(): pl.pallas_call(functools.partial(exchange_kernel, rows, cols), out_shape=...]
where the time goes in v3:
time: 80.6 us; the launch traced here: 80.4 us
  Pallas kernels  75.3 us (93%)
  local copies, waits for them, and re-layouts  4.42 us (5%)
    pallas_call x1, Pallas kernels, exchange(): pl.pallas_call(functools.partial(exchange_kernel, rows, cols), out_shape=...  67.1 us
    pallas_call x1, Pallas kernels, parent(): pl.pallas_call(parent_kernel, out_shape=jax.ShapeDtypeStruct((SKEL // 2,...  8.22 us
    unnamed x12, local copies, waits for them, and re-layouts  4.36 us

profile of v3, /device:TPU:13, one launch (start us, length us, event | category | flops | bytes accessed | tf_op | source)
XLA Modules:
  0.0 80.4 jit_solution(16324738527356731861)
XLA Ops:
  0.6 0.0 copy-start.4
  0.6 0.0 copy-start
  0.7 0.1 conditional.1
  0.8 0.5 copy-done.4
  1.3 0.3 copy-done
  1.6 67.1 %exchange.1 = (f32[384,384]{1,0:T(8,128)S(1)}, f32[2,128,256]{2,1,0:T(8,128)S(1)}, f32[2,128,256]{2,1,0:T(8,128)S(1)}, f32[128,256]{1,0:T(8,128)S(1)}, f32[256,128]{1,0:T(8,128)S(1)}) custom-call(s32[1,16]{1,0:T(1,128)S(1)} %copy-done.4, f32[4,512,512]{2,1,0:T(8,128)} %bitcast.10, f32[512,512]{1,0:T(8,128)} %bitcast.12, f32[256,256]{1,0:T(8,128)S(1)} %bitcast.6, ...), custom_call_target="tpu_custom_call" | custom-call | tf_op jit(solution)/shard_map/exchange/pallas_call | solution.py:456
  68.7 0.0 copy-start.1
  68.7 0.7 copy-done.1
  69.4 0.0 copy-start.2
  69.4 0.7 copy-done.2
  70.1 0.0 copy-start.3
  70.1 0.7 copy-done.3
  70.7 8.2 %parent.1 = f32[64,128]{1,0:T(8,128)} custom-call(f32[256,256]{1,0:T(8,128)} %bitcast.7, f32[256,256]{1,0:T(8,128)} %bitcast.8, f32[256,128]{1,0:T(8,128)} %copy-done.3, f32[256,256]{1,0:T(8,128)} %bitcast.5), custom_call_target="tpu_custom_call" | custom-call | tf_op jit(solution)/shard_map/parent/pallas_call | solution.py:506
  79.0 0.8 %copy.13 = f32[384,384]{1,0:T(8,128)} copy(f32[384,384]{1,0:T(8,128)S(1)} %get-tuple-element.30) | data formatting | bytes 1179648
  79.8 0.7 copy.14
  (2 shorter events, 0.1 us)
Async XLA Ops:
  0.6 0.7 copy-start.4
  0.6 1.0 %copy-start = (f32[1,256,256]{2,1,0:T(8,128)S(1)}, f32[1,256,256]{2,1,0:T(8,128)}, u32[]{:S(2)}) copy-start(f32[1,256,256]{2,1,0:T(8,128)} %param.8) | copy-start | bytes 786436
  68.7 0.7 copy-start.1
  69.4 0.7 copy-start.2
  70.1 0.7 copy-start.3

commit v4 on v3

--- a/solution.py
+++ b/solution.py
@@ -182,6 +182,7 @@
     upper_half[...] = upper_ref[:, SKEL:]
     row_basis_ref[...] = jnp.where(holder == col, upper_ref[:, SKEL:], 0.0)
     table[...] = jnp.zeros_like(table)
+    incoming[...] = jnp.zeros_like(incoming)
     diag_ref[...] = jnp.zeros_like(diag_ref)
     for lo in range(0, red - BLK, BLK):
         factor_ref[lo : lo + BLK, lo + BLK :] = jnp.zeros((BLK, red - lo - BLK), F32)
@@ -339,8 +340,13 @@
             outgoing.at[other], incoming.at[d], tile_send.at[d], tile_recv.at[d], row, other
         )
 
+    def wanted(c):
+        return (holder + parent_reach >= c) & (holder <= c + parent_reach)
+
     for d in range(1, cols):
-        send_tile(d).start()
+        @pl.when(wanted(lax.rem(col + d, cols)))
+        def _():
+            send_tile(d).start()
 
     @pl.when((col > 1) & (col < cols - 1))
     def _():
@@ -348,7 +354,10 @@
 
     total = outgoing[col]
     for d in range(1, cols):
-        send_tile(d).wait_recv()
+        @pl.when(wanted(col))
+        def _():
+            send_tile(d).wait_recv()
+
         total = total + incoming[d]
     strip_ref[...] = total
     merged_ref[parity] = total
@@ -422,7 +431,10 @@
         def _():
             to_diag(d).wait_send()
     for d in range(1, cols):
-        send_tile(d).wait_send()
+        @pl.when(wanted(lax.rem(col + d, cols)))
+        def _():
+            send_tile(d).wait_send()
+
     for k in range(CHUNKS):
         @pl.when(col < cols - 1)
         def _():

time: 80.6 us -> 80.6 us (level)
  no operation moved by 1% of the time
where the time goes in v4:
time: 80.6 us; the launch traced here: 80.4 us
  Pallas kernels  75.3 us (93%)
  local copies, waits for them, and re-layouts  4.42 us (5%)
    pallas_call x1, Pallas kernels, exchange(): pl.pallas_call(functools.partial(exchange_kernel, rows, cols), out_shape=...  67.1 us
    pallas_call x1, Pallas kernels, parent(): pl.pallas_call(parent_kernel, out_shape=jax.ShapeDtypeStruct((SKEL // 2,...  8.22 us
    unnamed x12, local copies, waits for them, and re-layouts  4.36 us

profile of v4, /device:TPU:13, one launch (start us, length us, event | category | flops | bytes accessed | tf_op | source)
XLA Modules:
  0.0 80.4 jit_solution(274703798250897206)
XLA Ops:
  0.6 0.0 copy-start.4
  0.6 0.0 copy-start
  0.7 0.1 conditional.1
  0.8 0.5 copy-done.4
  1.3 0.3 copy-done
  1.6 67.1 %exchange.1 = (f32[384,384]{1,0:T(8,128)S(1)}, f32[2,128,256]{2,1,0:T(8,128)S(1)}, f32[2,128,256]{2,1,0:T(8,128)S(1)}, f32[128,256]{1,0:T(8,128)S(1)}, f32[256,128]{1,0:T(8,128)S(1)}) custom-call(s32[1,16]{1,0:T(1,128)S(1)} %copy-done.4, f32[4,512,512]{2,1,0:T(8,128)} %bitcast.10, f32[512,512]{1,0:T(8,128)} %bitcast.12, f32[256,256]{1,0:T(8,128)S(1)} %bitcast.6, ...), custom_call_target="tpu_custom_call" | custom-call | tf_op jit(solution)/shard_map/exchange/pallas_call | solution.py:468
  68.7 0.0 copy-start.1
  68.7 0.7 copy-done.1
  69.4 0.0 copy-start.2
  69.4 0.7 copy-done.2
  70.1 0.0 copy-start.3
  70.1 0.7 copy-done.3
  70.8 8.2 %parent.1 = f32[64,128]{1,0:T(8,128)} custom-call(f32[256,256]{1,0:T(8,128)} %bitcast.7, f32[256,256]{1,0:T(8,128)} %bitcast.8, f32[256,128]{1,0:T(8,128)} %copy-done.3, f32[256,256]{1,0:T(8,128)} %bitcast.5), custom_call_target="tpu_custom_call" | custom-call | tf_op jit(solution)/shard_map/parent/pallas_call | solution.py:518
  79.0 0.8 %copy.13 = f32[384,384]{1,0:T(8,128)} copy(f32[384,384]{1,0:T(8,128)S(1)} %get-tuple-element.30) | data formatting | bytes 1179648
  79.8 0.7 copy.14
  (2 shorter events, 0.1 us)
Async XLA Ops:
  0.6 0.7 copy-start.4
  0.6 1.0 %copy-start = (f32[1,256,256]{2,1,0:T(8,128)S(1)}, f32[1,256,256]{2,1,0:T(8,128)}, u32[]{:S(2)}) copy-start(f32[1,256,256]{2,1,0:T(8,128)} %param.8) | copy-start | bytes 786436
  68.7 0.7 copy-start.1
  69.4 0.7 copy-start.2
  70.1 0.7 copy-start.3
